TPU v7x, 32 devices: a whole 2x2x4 slice. The times are simulated.
32 devices in a mesh: leaf: 4 (over y, x), blk: 8 (over z, core).
Axes of the slice: x: 2, y: 2, z: 4, core: 2. Of those that a mesh axis runs over, the one named last changes fastest.
Arguments:
- diag_blocks: float32 [4, 512, 512], P('leaf'), as said below
- panel: float32 [4, 32, 256, 512], P('leaf', 'blk'), may hold values from -1.2 to 1.2
- local_targets: bfloat16 [4, 640, 256, 256], P('leaf', 'blk'), may hold values from -6 to 6
- local_pairs: int32 [4, 640, 2], P('leaf', 'blk'), may hold values from -1 to 31, as said below
- top_targets: bfloat16 [8, 16, 256, 256], P('blk', 'leaf'), may hold values from -6 to 6
- top_pairs: int32 [8, 16, 2], P('blk'), may hold values from 0 to 63
- top_pattern: int32 [4, 64], P('leaf'), may hold values from -1 to 31, as said below
Outputs:
- panel_factor: bfloat16 [4, 32, 256, 512], P('leaf', 'blk')
- local_updated: bfloat16 [4, 640, 256, 256], P('leaf', 'blk')
- top_updated: bfloat16 [8, 16, 256, 256], P('blk', 'leaf')
Inputs may be any that keep to these rules, and one draw needn't show every extreme that they name: Each diag_blocks[g] is symmetric positive definite with smallest eigenvalue 0.5 or more. `local_pairs`: empty slots hold -1 in both columns; on each device the live slots come first; some device has all 80 slots live. `top_pattern`: in each group every panel row 0 to 31 stands at exactly one ancestor row; the other ancestor rows hold -1.
All inputs are finite; a program needn't handle non-finite values.
Results may differ from a plain program's by a relative error of at most 0.014.
Values may be sent and summed in bfloat16 or wider, within the bound.
A program may use at most 192 MiB of HBM per device.

v0:
```python
import functools

import jax
import jax.numpy as jnp
from jax import lax
from jax.experimental import pallas as pl
from jax.experimental.pallas import tpu as pltpu
from jax.sharding import PartitionSpec as P

NB = 128
HI = lax.Precision.HIGHEST
VMEM_LIMIT = 56 * 1024 * 1024


def mm(a, b, contract, precision=HI):
    return lax.dot_general(
        a, b, ((contract[:1], contract[1:]), ((), ())),
        precision=precision, preferred_element_type=jnp.float32,
    )


def eliminate(block, inv_ref):
    groups = NB // 8
    d = [block[8 * g:8 * g + 8, :] for g in range(groups)]
    row = lax.broadcasted_iota(jnp.int32, (8, NB), 0)
    col = lax.broadcasted_iota(jnp.int32, (8, NB), 1)
    e = [jnp.where(row + 8 * g == col, 1.0, 0.0).astype(jnp.float32) for g in range(groups)]
    for j in range(NB):
        g, r = divmod(j, 8)
        drow = d[g][r:r + 1, :]
        erow = e[g][r:r + 1, :]
        pivot = jnp.broadcast_to(drow[:, j:j + 1], (1, NB))
        inv_ref[j:j + 1, :] = erow * lax.rsqrt(pivot)
        inverse = 1.0 / pivot
        dscaled = drow * inverse
        escaled = erow * inverse
        for h in range(g if r < 7 else g + 1, groups):
            factor = jnp.broadcast_to(d[h][:, j:j + 1], (8, NB))
            d[h] = d[h] - factor * dscaled
            e[h] = e[h] - factor * escaled


def factor_step(last, s_ref, a_ref, x_ref, *rest):
    inv_ref = rest[-1]
    eliminate(s_ref[0:NB, 0:NB], inv_ref)
    inverse = inv_ref[...]
    x = mm(a_ref[:, 0:NB], inverse, (1, 1))
    x_ref[...] = x.astype(x_ref.dtype)
    if not last:
        s_next, a_next = rest[:2]
        upper = mm(inverse, s_ref[0:NB, NB:], (1, 0))
        s_next[...] = s_ref[NB:, NB:] - mm(upper, upper, (0, 0))
        a_next[...] = a_ref[:, NB:] - mm(x, upper, (1, 0))


def run_factor_step(s, a):
    order, rows = s.shape[0], a.shape[0]
    last = order == NB
    out = [jax.ShapeDtypeStruct((rows, NB), jnp.bfloat16)]
    if not last:
        out += [
            jax.ShapeDtypeStruct((order - NB, order - NB), jnp.float32),
            jax.ShapeDtypeStruct((rows, order - NB), jnp.float32),
        ]
    vmem = pl.BlockSpec(memory_space=pltpu.VMEM)
    return pl.pallas_call(
        functools.partial(factor_step, last),
        out_shape=out,
        in_specs=[vmem, vmem],
        out_specs=[vmem] * len(out),
        scratch_shapes=[pltpu.VMEM((NB, NB), jnp.float32)],
        compiler_params=pltpu.CompilerParams(vmem_limit_bytes=VMEM_LIMIT),
        cost_estimate=pl.CostEstimate(flops=20_000_000_000, bytes_accessed=8_000_000, transcendentals=0),
        name="factor_step",
    )(s, a)


def product(refs, p, q):
    left = jnp.concatenate([ref[p] for ref in refs], axis=1)
    right = jnp.concatenate([ref[q] for ref in refs], axis=1)
    return mm(left, right, (1, 1), None)


def top_kernel(per_step, pairs, *refs):
    slices, out = refs[:-1], refs[-1]
    base = pl.program_id(0) * per_step
    for s in range(per_step):
        p, q = pairs[0, base + s], pairs[1, base + s]
        present = (p >= 0) & (q >= 0)

        @pl.when(present)
        def _():
            out[s] = product(slices, p, q).astype(out.dtype)

        @pl.when(jnp.logical_not(present))
        def _():
            out[s] = jnp.zeros(out.shape[1:], out.dtype)


def local_kernel(per_step, pairs, *refs):
    slices, target, out = refs[:-2], refs[-2], refs[-1]
    base = pl.program_id(0) * per_step
    for s in range(per_step):
        p, q = pairs[0, base + s], pairs[1, base + s]

        @pl.when(p >= 0)
        def _():
            fresh = target[s].astype(jnp.float32) - product(slices, p, q)
            out[s] = fresh.astype(out.dtype)

        @pl.when(p < 0)
        def _():
            out[s] = target[s]


def run_pairs(kernel, pairs, slices, targets, count, per_step, name):
    rows, width, depth = slices[0].shape
    whole = pl.BlockSpec((rows, width, depth), lambda i, pairs: (0, 0, 0), pipeline_mode=pl.Buffered(1))
    block = pl.BlockSpec((per_step, width, width), lambda i, pairs: (i, 0, 0))
    extra = [] if targets is None else [targets]
    return pl.pallas_call(
        functools.partial(kernel, per_step),
        grid_spec=pltpu.PrefetchScalarGridSpec(
            num_scalar_prefetch=1,
            grid=(count // per_step,),
            in_specs=[whole] * len(slices) + [block] * len(extra),
            out_specs=block,
        ),
        out_shape=jax.ShapeDtypeStruct((count, width, width), jnp.bfloat16),
        compiler_params=pltpu.CompilerParams(vmem_limit_bytes=VMEM_LIMIT),
        cost_estimate=pl.CostEstimate(
            flops=2 * count * width * width * depth * len(slices),
            bytes_accessed=4 * count * width * width,
            transcendentals=0,
        ),
        name=name,
    )(pairs, *slices, *extra)


def on_device(diag_blocks, panel, local_targets, local_pairs, top_targets, top_pairs, top_pattern):
    s = diag_blocks[0]
    count, width, columns = panel.shape[1:]
    a = panel[0].reshape(count * width, columns)
    pattern = top_pattern[0]
    ancestors = jnp.arange(pattern.shape[0], dtype=jnp.int32)

    def lookup(ids):
        return jnp.sum(jnp.where(ids[:, None] == ancestors[None, :], pattern[None, :], 0), axis=1)

    positions = jnp.stack([lookup(top_pairs[0, :, 0]), lookup(top_pairs[0, :, 1])])
    pairs = local_pairs[0].T

    own, slices = [], []
    while True:
        x, *state = run_factor_step(s, a)
        x = x.reshape(count, width, NB)
        own.append(x)
        slices.append(lax.all_gather(x, "blk", axis=0, tiled=True))
        if not state:
            break
        s, a = state
    panel_out = jnp.concatenate(own, axis=2)[None]

    partial = run_pairs(top_kernel, positions, slices, None, top_pairs.shape[1], 4, "top_products")
    summed = lax.psum_scatter(partial, "leaf", scatter_dimension=0, tiled=True).astype(jnp.float32)
    updated = run_pairs(
        local_kernel, pairs, slices, local_targets[0], local_targets.shape[1], 8, "local_updates"
    )
    top_out = (top_targets[0].astype(jnp.float32) - summed).astype(jnp.bfloat16)[None]
    return (panel_out, updated[None], top_out)


def solution(mesh):
    in_specs = (
        P("leaf", None, None),
        P("leaf", "blk", None, None),
        P("leaf", "blk", None, None),
        P("leaf", "blk", None),
        P("blk", "leaf", None, None),
        P("blk", None, None),
        P("leaf", None),
    )
    out_specs = (
        P("leaf", "blk", None, None),
        P("leaf", "blk", None, None),
        P("blk", "leaf", None, None),
    )
    return jax.shard_map(
        on_device, mesh=mesh, in_specs=in_specs, out_specs=out_specs, check_vma=False
    )
```

profile of v0, /device:TPU:0, one launch (start us, length us, event | category | flops | bytes accessed | tf_op | source)
XLA Modules:
  0.0 197.8 jit_solution(16115798619650289988)
XLA Ops:
  7.2 0.0 all-gather.5.cloned.1.call-start
  7.2 16.3 %factor_step.4 = (bf16[1024,128]{1,0:T(8,128)(2,1)}, f32[384,384]{1,0:T(8,128)}, f32[1024,384]{1,0:T(8,128)}) custom-call(f32[512,512]{1,0:T(8,128)} %bitcast.40, f32[1024,512]{1,0:T(8,128)} %bitcast.39), custom_call_target="tpu_custom_call" | custom-call | flops 20000000000 | bytes 8000000 | tf_op jit(solution)/shard_map/factor_step/pallas_call | solution.py:66
  23.5 0.0 all-gather.5.cloned.1.call-update
  23.5 0.2 all-gather.7.cloned.1.call-start
  23.7 15.2 %factor_step.5 = (bf16[1024,128]{1,0:T(8,128)(2,1)}, f32[256,256]{1,0:T(8,128)}, f32[1024,256]{1,0:T(8,128)}) custom-call(f32[384,384]{1,0:T(8,128)} %get-tuple-element.13.s_ref, f32[1024,384]{1,0:T(8,128)} %get-tuple-element.14.a_ref), custom_call_target="tpu_custom_call" | custom-call | flops 20000000000 | bytes 8000000 | tf_op jit(solution)/shard_map/factor_step/pallas_call | solution.py:66
  39.0 0.0 all-gather.7.cloned.1.call-update
  39.0 0.0 all-gather.9.cloned.1.call-start
  39.0 14.6 %factor_step.6 = (bf16[1024,128]{1,0:T(8,128)(2,1)}, f32[128,128]{1,0:T(8,128)}, f32[1024,128]{1,0:T(8,128)}) custom-call(f32[256,256]{1,0:T(8,128)} %get-tuple-element.16.s_ref, f32[1024,256]{1,0:T(8,128)} %get-tuple-element.17.a_ref), custom_call_target="tpu_custom_call" | custom-call | flops 20000000000 | bytes 8000000 | tf_op jit(solution)/shard_map/factor_step/pallas_call | solution.py:66
  53.6 0.0 all-gather.9.cloned.1.call-update
  53.6 0.3 all-gather.11.cloned.1.call-start
  53.9 0.0 copy-start.5
  53.9 0.0 copy-start.6
  53.9 13.1 %factor_step.7 = bf16[1024,128]{1,0:T(8,128)(2,1)} custom-call(f32[128,128]{1,0:T(8,128)} %get-tuple-element.19.s_ref, f32[1024,128]{1,0:T(8,128)} %get-tuple-element.20.a_ref), custom_call_target="tpu_custom_call" | custom-call | flops 20000000000 | bytes 8000000 | tf_op jit(solution)/shard_map/factor_step/pallas_call | solution.py:66
  67.0 0.0 all-gather.11.cloned.1.call-update
  67.0 0.0 reduce-scatter.2.cloned.1.call-start
  67.1 0.0 copy-done.5
  67.1 0.0 copy-done.6
  67.1 0.2 select_reduce_fusion.1
  67.3 0.6 pad_add_fusion.pairs
  67.8 0.0 all-gather.5.cloned.1.call-done.refs_0_
  67.8 18.0 %all-gather.7.cloned.1.call-done.refs_1_ = bf16[32,256,128]{2,1,0:T(8,128)(2,1)} async-done(((bf16[4,256,128]{2,1,0:T(8,128)(2,1)}), bf16[32,256,128]{2,1,0:T(8,128)(2,1)}) %all-gather.7.cloned.1.call-update) | async-done | bytes 2097168 | tf_op jit(solution)/shard_map/all_gather | solution.py:158
  85.8 30.8 %all-gather.9.cloned.1.call-done.refs_2_ = bf16[32,256,128]{2,1,0:T(8,128)(2,1)} async-done(((bf16[4,256,128]{2,1,0:T(8,128)(2,1)}), bf16[32,256,128]{2,1,0:T(8,128)(2,1)}) %all-gather.9.cloned.1.call-update) | async-done | bytes 2097168 | tf_op jit(solution)/shard_map/all_gather | solution.py:158
  116.6 30.7 %all-gather.11.cloned.1.call-done.refs_3_ = bf16[32,256,128]{2,1,0:T(8,128)(2,1)} async-done(((bf16[4,256,128]{2,1,0:T(8,128)(2,1)}), bf16[32,256,128]{2,1,0:T(8,128)(2,1)}) %all-gather.11.cloned.1.call-update) | async-done | bytes 2097168 | tf_op jit(solution)/shard_map/all_gather | solution.py:158
  147.3 6.8 %top_products.1 = bf16[16,256,256]{2,1,0:T(8,128)(2,1)} custom-call(s32[2,16]{1,0:T(2,128)} %pad_add_fusion.pairs, bf16[32,256,128]{2,1,0:T(8,128)(2,1)} %all-gather.5.cloned.1.call-done.refs_0_, bf16[32,256,128]{2,1,0:T(8,128)(2,1)} %all-gather.7.cloned.1.call-done.refs_1_, bf16[32,256,128]{2,1,0:T(8,128)(2,1)} %all-gather.9.cloned.1.call-done.refs_2_, ...), custom_call_target="tpu_custom_call" | custom-call | flops 1073741824 | bytes 4194304 | tf_op jit(solution)/shard_map/top_products/pallas_call | solution.py:121
  154.1 0.0 copy-start
  154.1 0.0 copy-start.1
  154.1 0.0 copy-start.2
  154.1 0.0 copy-start.3
  154.1 0.0 reduce-scatter.2.cloned.1.call-update
  154.1 0.9 copy-done
  155.0 0.1 copy-done.1
  155.1 0.1 copy-done.2
  155.2 0.1 copy-done.3
  155.3 1.1 maximum_bitcast_fusion
  156.4 0.0 copy-start.4
  156.4 18.2 %local_updates.1 = bf16[80,256,256]{2,1,0:T(8,128)(2,1)} custom-call(s32[2,80]{1,0:T(2,128)} %bitcast.37, bf16[32,256,128]{2,1,0:T(8,128)(2,1)} %all-gather.5.cloned.1.call-done.refs_0_, bf16[32,256,128]{2,1,0:T(8,128)(2,1)} %all-gather.7.cloned.1.call-done.refs_1_, bf16[32,256,128]{2,1,0:T(8,128)(2,1)} %all-gather.9.cloned.1.call-done.refs_2_, ...), custom_call_target="tpu_custom_call" | custom-call | flops 5368709120 | bytes 20971520 | tf_op jit(solution)/shard_map/local_updates/pallas_call | solution.py:121
  174.6 14.8 %reduce-scatter.2.cloned.1.call-done = bf16[4,256,256]{2,1,0:T(8,128)(2,1)} async-done(((bf16[16,256,256]{2,1,0:T(8,128)(2,1)}), bf16[4,256,256]{2,1,0:T(8,128)(2,1)}) %reduce-scatter.2.cloned.1.call-update) | async-done | bytes 524304 | tf_op jit(solution)/shard_map/reduce_scatter | solution.py:165
  189.3 0.0 copy-done.4
  189.3 2.0 fusion.1
  (1 shorter events, 0.0 us)
Async XLA Ops:
  7.2 60.7 %all-gather.5.cloned.1.call-start = ((), (), s32[]{:S(2)}) async-start(), calls=%async_computation.1 | async-start | bytes 2359296 | tf_op jit(solution)/shard_map/all_gather | solution.py:158
  23.5 62.3 %all-gather.7.cloned.1.call-start = ((), (), s32[]{:S(2)}) async-start(), calls=%async_computation.2 | async-start | bytes 2359296 | tf_op jit(solution)/shard_map/all_gather | solution.py:158
  39.0 77.7 %all-gather.9.cloned.1.call-start = ((), (), s32[]{:S(2)}) async-start(), calls=%async_computation.3 | async-start | bytes 2359296 | tf_op jit(solution)/shard_map/all_gather | solution.py:158
  53.6 93.7 %all-gather.11.cloned.1.call-start = ((), (), s32[]{:S(2)}) async-start(), calls=%async_computation.4 | async-start | bytes 2359296 | tf_op jit(solution)/shard_map/all_gather | solution.py:158
  53.9 13.2 %copy-start.5 = (s32[1,16,2]{1,2,0:T(2,128)S(1)}, s32[1,16,2]{1,2,0:T(2,128)}, u32[]{:S(2)}) copy-start(s32[1,16,2]{1,2,0:T(2,128)} %param.12) | copy-start | bytes 388
  53.9 13.2 %copy-start.6 = (s32[1,64]{1,0:T(1,128)S(1)}, s32[1,64]{1,0:T(1,128)}, u32[]{:S(2)}) copy-start(s32[1,64]{1,0:T(1,128)} %param.13) | copy-start | bytes 772
  67.0 122.3 %reduce-scatter.2.cloned.1.call-start = ((), (), s32[]{:S(2)}) async-start(), calls=%async_computation.5 | async-start | bytes 2621440 | tf_op jit(solution)/shard_map/reduce_scatter | solution.py:165
  154.1 0.9 copy-start
  154.1 1.0 copy-start.1
  154.1 1.1 copy-start.2
  154.1 1.2 copy-start.3
  156.4 33.0 %copy-start.4 = (bf16[1,4,256,256]{3,2,1,0:T(8,128)(2,1)S(1)}, bf16[1,4,256,256]{3,2,1,0:T(8,128)(2,1)}, u32[]{:S(2)}) copy-start(bf16[1,4,256,256]{3,2,1,0:T(8,128)(2,1)} %param.11) | copy-start | bytes 1572868
Sparse Core Ops, SparseCore 0:
  23.6 31.8 all-gather.4
  57.1 28.6 all-gather.6
  88.0 28.5 all-gather.8
  118.7 28.5 all-gather.10
  154.3 35.0 reduce-scatter.1
where the time goes:
time: 198 us
  waiting for transfers between devices  94.3 us (48%)
  Pallas kernels  84.1 us (42%)
  between operations  13.8 us (7%)
  other arithmetic  3.81 us (2%)
    all_gather x4, waiting for transfers between devices, on_device(): slices.append(lax.all_gather(x, 'blk', axis=0, tiled=True))  79.4 us
    pallas_call x4, Pallas kernels, run_factor_step(): pl.pallas_call(functools.partial(factor_step, last), out_shape=out, in_sp...  59.1 us
    pallas_call x2, Pallas kernels, run_pairs(): pl.pallas_call(functools.partial(kernel, per_step), grid_spec=pltpu.Prefe...  25 us
    reduce_scatter x1, waiting for transfers between devices, on_device(): lax.psum_scatter(partial, 'leaf', scatter_dimension=0, tiled=True)  14.8 us
  transfers between devices with their start and end apart: 5, of which 4 were waited for; matrix products, arithmetic and copies ran while one was open for 1% of the time, Pallas kernels for 31%

commit v1 on v0

v1 whole, which is shorter than its diff:
```python
import functools

import jax
import jax.numpy as jnp
from jax import lax
from jax.experimental import pallas as pl
from jax.experimental.pallas import tpu as pltpu
from jax.sharding import PartitionSpec as P

NB = 128
MESH = pl.DeviceIdType.MESH
HI = lax.Precision.HIGHEST
VMEM_LIMIT = 56 * 1024 * 1024


def mm(a, b, contract, precision=HI):
    return lax.dot_general(
        a, b, ((contract[:1], contract[1:]), ((), ())),
        precision=precision, preferred_element_type=jnp.float32,
    )


def eliminate(block, inv_ref, midway):
    d = block
    row = lax.broadcasted_iota(jnp.int32, (NB, NB), 0)
    col = lax.broadcasted_iota(jnp.int32, (NB, NB), 1)
    e = jnp.where(row == col, 1.0, 0.0).astype(jnp.float32)
    top = 0
    for j in range(NB):
        if j - top == 16:
            d, e, top = d[16:], e[16:], j
        if j == NB // 2:
            midway()
        r = j - top
        drow = d[r:r + 1, :]
        erow = e[r:r + 1, :]
        pivot = jnp.broadcast_to(drow[:, j:j + 1], (1, NB))
        inv_ref[j:j + 1, :] = erow * lax.rsqrt(pivot)
        inverse = 1.0 / pivot
        factor = jnp.broadcast_to(d[:, j:j + 1], d.shape)
        d = d - factor * (drow * inverse)
        e = e - factor * (erow * inverse)


def factor_kernel(
    stages, s_in, a_in, x_all, panel_out, s_ref, a_ref, inv_ref, x_ref,
    own_sem, net_send, down_send, net_recv, part_send, part_recv,
):
    leaf, blk = lax.axis_index("leaf"), lax.axis_index("blk")
    z, core = lax.div(blk, 2), lax.rem(blk, 2)
    partner = 2 * z + 1 - core
    slices, count, width = x_ref.shape[:3]
    last = stages - 1

    barrier = pltpu.get_barrier_semaphore()

    def signal(target):
        pl.semaphore_signal(barrier, inc=1, device_id=(leaf, target), device_id_type=MESH)

    signal(partner)

    @pl.when(z < last)
    def _():
        signal(blk + 2)

    @pl.when(z > 0)
    def _():
        signal(blk - 2)

    def chunk(q, origin, lane):
        return x_all.at[q, pl.ds((2 * origin + lane) * count, count)]

    def remote(src, q, origin, lane, send, recv, target):
        return pltpu.make_async_remote_copy(
            src_ref=src, dst_ref=chunk(q, origin, lane), send_sem=send, recv_sem=recv,
            device_id=(leaf, target), device_id_type=MESH,
        )

    def net(src, q, origin, target):
        return remote(src, q, origin, core, net_send.at[q, origin], net_recv.at[q, origin], target)

    def down_own(q):
        return remote(x_ref.at[q], q, z, core, down_send.at[q], net_recv.at[q, z], blk - 2)

    def across(src, q, origin):
        return remote(src, q, origin, core, part_send.at[q, origin], part_recv.at[q, origin], partner)

    def local(q):
        return pltpu.make_async_copy(x_ref.at[q], chunk(q, z, core), own_sem.at[q])

    def send_own(q):
        @pl.when(z < last)
        def _():
            net(x_ref.at[q], q, z, blk + 2).start()

        @pl.when(z > 0)
        def _():
            down_own(q).start()

        across(x_ref.at[q], q, z).start()
        local(q).start()

    def forward(q, hop):
        above, below = z - hop, z + hop

        @pl.when(above >= 0)
        def _():
            held = chunk(q, above, core)
            net(held, q, above, blk).wait_recv()

            @pl.when(z < last)
            def _():
                net(held, q, above, blk + 2).start()

            across(held, q, above).start()

        @pl.when(below <= last)
        def _():
            held = chunk(q, below, core)
            net(held, q, below, blk).wait_recv()

            @pl.when(z > 0)
            def _():
                net(held, q, below, blk - 2).start()

            across(held, q, below).start()

    def forwards(tick):
        for q in range(slices):
            hop = tick - 2 * q
            if 1 <= hop <= last:
                forward(q, hop)

    for q in range(slices):
        s_now, a_now = (s_in, a_in) if q == 0 else (s_ref, a_ref)
        at = q * NB
        eliminate(s_now[at:at + NB, at:at + NB], inv_ref, lambda: forwards(2 * q - 1))
        inverse = inv_ref[...]
        x = mm(a_now[:, at:at + NB], inverse, (1, 1))
        rounded = x.astype(x_ref.dtype)
        x_ref[q] = rounded.reshape(count, width, NB)
        panel_out[:, at:at + NB] = rounded
        if q == 0:
            pl.semaphore_wait(barrier, 1 + jnp.minimum(z, 1) + jnp.minimum(last - z, 1))

        send_own(q)
        forwards(2 * q)
        if q < slices - 1:
            upper = mm(inverse, s_now[at:at + NB, at + NB:], (1, 0))
            s_ref[at + NB:, at + NB:] = s_now[at + NB:, at + NB:] - mm(upper, upper, (0, 0))
            a_ref[:, at + NB:] = a_now[:, at + NB:] - mm(x, upper, (1, 0))

    for tick in range(2 * slices - 1, 2 * slices - 1 + last):
        forwards(tick)

    for q in range(slices):
        local(q).wait()

        @pl.when(z > 0)
        def _():
            down_own(q).wait_send()

        for origin in range(stages):
            held = chunk(q, origin, core)
            across(held, q, origin).wait_send()
            remote(
                held, q, origin, 1 - core,
                part_send.at[q, origin], part_recv.at[q, origin], partner,
            ).wait_recv()

            @pl.when(((origin <= z) & (z < last)) | ((origin > z) & (z > 0)))
            def _():
                net(held, q, origin, blk).wait_send()


def run_factor(s, a, count, parts):
    order, rows = s.shape[0], a.shape[0]
    slices, stages, width = order // NB, parts // 2, rows // count
    vmem = pl.BlockSpec(memory_space=pltpu.VMEM)
    dma = pltpu.SemaphoreType.DMA
    return pl.pallas_call(
        functools.partial(factor_kernel, stages),
        out_shape=[
            jax.ShapeDtypeStruct((slices, parts * count, width, NB), jnp.bfloat16),
            jax.ShapeDtypeStruct((rows, order), jnp.bfloat16),
        ],
        in_specs=[vmem, vmem],
        out_specs=[pl.BlockSpec(memory_space=pl.ANY), vmem],
        scratch_shapes=[
            pltpu.VMEM((order, order), jnp.float32),
            pltpu.VMEM((rows, order), jnp.float32),
            pltpu.VMEM((NB, NB), jnp.float32),
            pltpu.VMEM((slices, count, width, NB), jnp.bfloat16),
            dma((slices,)),
            dma((slices, stages)),
            dma((slices,)),
            dma((slices, stages)),
            dma((slices, stages)),
            dma((slices, stages)),
        ],
        compiler_params=pltpu.CompilerParams(
            vmem_limit_bytes=VMEM_LIMIT, collective_id=0, has_side_effects=True
        ),
        cost_estimate=pl.CostEstimate(flops=80_000_000_000, bytes_accessed=16_000_000, transcendentals=0),
        name="factor_and_gather",
    )(s, a)


def product(rows, p, q):
    slices = range(rows.shape[0])
    left = jnp.concatenate([rows[k, jnp.maximum(p, 0)] for k in slices], axis=1)
    right = jnp.concatenate([rows[k, jnp.maximum(q, 0)] for k in slices], axis=1)
    live = (p >= 0) & (q >= 0)
    return jnp.where(live, mm(left, right, (1, 1), None), 0.0)


def top_kernel(pairs, rows, *outs):
    per_out = outs[0].shape[0]
    for k in range(len(outs)):
        for s in range(per_out):
            at = k * per_out + s
            outs[k][s] = product(rows, pairs[0, at], pairs[1, at]).astype(outs[k].dtype)


def run_top(pairs, rows, shares, width):
    per_out = pairs.shape[1] // shares
    vmem = pl.BlockSpec(memory_space=pltpu.VMEM)
    shape = jax.ShapeDtypeStruct((per_out, width, width), jnp.bfloat16)
    return pl.pallas_call(
        top_kernel,
        in_specs=[pl.BlockSpec(memory_space=pltpu.SMEM), vmem],
        out_specs=[vmem] * shares,
        out_shape=[shape] * shares,
        compiler_params=pltpu.CompilerParams(vmem_limit_bytes=VMEM_LIMIT),
        cost_estimate=pl.CostEstimate(flops=1_000_000_000, bytes_accessed=10_000_000, transcendentals=0),
        name="top_products",
    )(pairs, rows)


def local_kernel(per_step, pairs, rows, target, out):
    base = pl.program_id(0) * per_step
    for s in range(per_step):
        fresh = target[s].astype(jnp.float32) - product(rows, pairs[0, base + s], pairs[1, base + s])
        out[s] = fresh.astype(out.dtype)


def run_local(pairs, rows, targets, per_step):
    count, width = targets.shape[:2]
    depth = rows.shape[0] * rows.shape[3]
    whole = pl.BlockSpec(rows.shape, lambda i, pairs: (0, 0, 0, 0), pipeline_mode=pl.Buffered(1))
    block = pl.BlockSpec((per_step, width, width), lambda i, pairs: (i, 0, 0))
    return pl.pallas_call(
        functools.partial(local_kernel, per_step),
        grid_spec=pltpu.PrefetchScalarGridSpec(
            num_scalar_prefetch=1,
            grid=(count // per_step,),
            in_specs=[whole, block],
            out_specs=block,
        ),
        out_shape=jax.ShapeDtypeStruct((count, width, width), jnp.bfloat16),
        compiler_params=pltpu.CompilerParams(vmem_limit_bytes=VMEM_LIMIT),
        cost_estimate=pl.CostEstimate(
            flops=2 * count * width * width * depth,
            bytes_accessed=4 * count * width * width,
            transcendentals=0,
        ),
        name="local_updates",
    )(pairs, rows, targets)


def on_device(leaves, parts, diag_blocks, panel, local_targets, local_pairs, top_targets, top_pairs, top_pattern):
    s = diag_blocks[0]
    count, width, columns = panel.shape[1:]
    a = panel[0].reshape(count * width, columns)
    pattern = top_pattern[0]
    ancestors = jnp.arange(pattern.shape[0], dtype=jnp.int32)

    def lookup(ids):
        return jnp.sum(jnp.where(ids[:, None] == ancestors[None, :], pattern[None, :], 0), axis=1)

    owners = lax.axis_index("leaf") ^ jnp.arange(leaves, dtype=jnp.int32)
    pairs_by_share = top_pairs[0].reshape(leaves, -1, 2)[owners].reshape(-1, 2)
    positions = jnp.stack([lookup(pairs_by_share[:, 0]), lookup(pairs_by_share[:, 1])])

    rows, panel_out = run_factor(s, a, count, parts)
    shares = run_top(positions, rows, leaves, width)
    arrived = [
        lax.ppermute(shares[m], "leaf", [(i, i ^ m) for i in range(leaves)])
        for m in range(1, leaves)
    ]
    updated = run_local(local_pairs[0].T, rows, local_targets[0], 8)
    summed = shares[0].astype(jnp.float32)
    for term in arrived:
        summed = summed + term.astype(jnp.float32)
    top_out = (top_targets[0].astype(jnp.float32) - summed).astype(jnp.bfloat16)[None]
    return (panel_out.reshape(panel.shape), updated[None], top_out)


def solution(mesh):
    in_specs = (
        P("leaf", None, None),
        P("leaf", "blk", None, None),
        P("leaf", "blk", None, None),
        P("leaf", "blk", None),
        P("blk", "leaf", None, None),
        P("blk", None, None),
        P("leaf", None),
    )
    out_specs = (
        P("leaf", "blk", None, None),
        P("leaf", "blk", None, None),
        P("blk", "leaf", None, None),
    )
    return jax.shard_map(
        functools.partial(on_device, mesh.shape["leaf"], mesh.shape["blk"]),
        mesh=mesh, in_specs=in_specs, out_specs=out_specs, check_vma=False
    )
```

time: 198 us -> 129 us (0.65)
  waiting for transfers between devices: 94.3 us -> 6.52 us
  Pallas kernels: 84.1 us -> 113 us
  between operations: 13.8 us -> 0.67 us
  starting transfers between devices: 0.61 us -> 3.5 us
    all_gather x4 -> x0, waiting for transfers between devices: 79.4 us -> none  [on_device(): slices.append(lax.all_gather(x, 'blk', axis=0, tiled=True))]
    pallas_call x6 -> x3, Pallas kernels: 84.1 us -> 113 us  [the longest x1 90.4 us: run_factor(): pl.pallas_call(functools.partial(factor_kernel, stages), out_shape=[jax.S...]
    reduce_scatter x1 -> x0, waiting for transfers between devices: 14.8 us -> none  [on_device(): lax.psum_scatter(partial, 'leaf', scatter_dimension=0, tiled=True)]
    ppermute x0 -> x3, waiting for transfers between devices: none -> 6.52 us  [on_device(): lax.ppermute(shares[m], 'leaf', [(i, i ^ m) for i in range(leaves)])]
    ppermute x0 -> x3, starting transfers between devices: none -> 3.5 us  [on_device(): lax.ppermute(shares[m], 'leaf', [(i, i ^ m) for i in range(leaves)])]
  transfers between devices with their start and end apart: 5 -> 3, of which waited for: 4 -> 1; matrix products, arithmetic and copies ran while one was open for 1% -> 0% of each run, Pallas kernels for 31% -> 13%
where the time goes in v1:
time: 129 us
  Pallas kernels  113 us (88%)
  waiting for transfers between devices  6.52 us (5%)
  starting transfers between devices  3.5 us (3%)
  other arithmetic  2.55 us (2%)
  local copies, waits for them, and re-layouts  2.42 us (2%)
    pallas_call x1, Pallas kernels, run_factor(): pl.pallas_call(functools.partial(factor_kernel, stages), out_shape=[jax.S...  90.4 us
    pallas_call x1, Pallas kernels, run_local(): pl.pallas_call(functools.partial(local_kernel, per_step), grid_spec=pltpu...  16.8 us
    ppermute x3, waiting for transfers between devices, on_device(): lax.ppermute(shares[m], 'leaf', [(i, i ^ m) for i in range(leaves)])  6.52 us
    pallas_call x1, Pallas kernels, run_top(): pl.pallas_call(top_kernel, in_specs=[pl.BlockSpec(memory_space=pltpu.SMEM...  5.72 us
    ppermute x3, starting transfers between devices, on_device(): lax.ppermute(shares[m], 'leaf', [(i, i ^ m) for i in range(leaves)])  3.5 us
  transfers between devices with their start and end apart: 3, of which 1 were waited for; matrix products, arithmetic and copies ran while one was open for 0% of the time, Pallas kernels for 13%

profile of v1, /device:TPU:0, one launch (start us, length us, event | category | flops | bytes accessed | tf_op | source)
XLA Modules:
  0.0 128.6 jit_solution(3366082549063390949)
XLA Ops:
  0.7 0.8 reshape_squeeze.7
  1.4 0.6 gather_fusion
  2.0 0.1 reshape.31
  2.1 0.8 select_reduce_fusion.1
  2.9 0.6 pad_add_fusion.pairs
  3.5 90.4 %factor_and_gather.1 = (bf16[4,32,256,128]{3,2,1,0:T(8,128)(2,1)}, bf16[1024,512]{1,0:T(8,128)(2,1)}) custom-call(f32[512,512]{1,0:T(8,128)} %bitcast.34, f32[1024,512]{1,0:T(8,128)} %bitcast.33), custom_call_target="tpu_custom_call" | custom-call | flops 80000000000 | bytes 16000000 | tf_op jit(solution)/shard_map/factor_and_gather/pallas_call | solution.py:181
  93.9 5.7 %top_products.1 = (bf16[4,256,256]{2,1,0:T(8,128)(2,1)}, bf16[4,256,256]{2,1,0:T(8,128)(2,1)}, bf16[4,256,256]{2,1,0:T(8,128)(2,1)}, bf16[4,256,256]{2,1,0:T(8,128)(2,1)}) custom-call(s32[2,16]{1,0:T(2,128)} %pad_add_fusion.pairs, bf16[4,32,256,128]{3,2,1,0:T(8,128)(2,1)} %get-tuple-element.10.rows), custom_call_target="tpu_custom_call" | custom-call | flops 1000000000 | bytes 10000000 | tf_op jit(solution)/shard_map/top_products/pallas_call | solution.py:229
  99.7 1.5 %collective-permute-start = (bf16[4,256,256]{2,1,0:T(8,128)(2,1)}, bf16[4,256,256]{2,1,0:T(8,128)(2,1)S(1)}, u32[]{:S(2)}, u32[]{:S(2)}) collective-permute-start(bf16[4,256,256]{2,1,0:T(8,128)(2,1)} %get-tuple-element.12), channel_id=1, source_target_pairs={{0,8},{8,0},{16,24},{24,16},{1,9},{9,1},{17,25},{25,17},{2,10},{10... | collective-permute-start | bytes 1572872 | tf_op jit(solution)/shard_map/ppermute | solution.py:288
  101.2 1.5 %collective-permute-start.1 = (bf16[4,256,256]{2,1,0:T(8,128)(2,1)}, bf16[4,256,256]{2,1,0:T(8,128)(2,1)S(1)}, u32[]{:S(2)}, u32[]{:S(2)}) collective-permute-start(bf16[4,256,256]{2,1,0:T(8,128)(2,1)} %get-tuple-element.13), channel_id=1, source_target_pairs={{0,16},{8,24},{16,0},{24,8},{1,17},{9,25},{17,1},{25,9},{2,18},{10... | collective-permute-start | bytes 1572872 | tf_op jit(solution)/shard_map/ppermute | solution.py:288
  102.7 0.5 collective-permute-start.2
  103.2 0.0 copy-start.1
  103.2 0.0 copy-start.2
  103.2 0.0 copy-start
  103.2 16.8 %local_updates.1 = bf16[80,256,256]{2,1,0:T(8,128)(2,1)} custom-call(s32[2,80]{1,0:T(2,128)} %bitcast.31, bf16[4,32,256,128]{3,2,1,0:T(8,128)(2,1)} %get-tuple-element.10.rows, bf16[80,256,256]{2,1,0:T(8,128)(2,1)} %bitcast.26), custom_call_target="tpu_custom_call" | custom-call | flops 5368709120 | bytes 20971520 | tf_op jit(solution)/shard_map/local_updates/pallas_call | solution.py:252
  120.0 0.0 collective-permute-done
  120.0 6.5 %collective-permute-done.1 = bf16[4,256,256]{2,1,0:T(8,128)(2,1)S(1)} collective-permute-done((bf16[4,256,256]{2,1,0:T(8,128)(2,1)}, bf16[4,256,256]{2,1,0:T(8,128)(2,1)S(1)}, u32[]{:S(2)}, u32[]{:S(2)}) %collective-permute-start.1) | collective-permute-done | bytes 524320 | tf_op jit(solution)/shard_map/ppermute | solution.py:288
  126.5 0.0 collective-permute-done.2
  126.5 0.0 copy-done.1
  126.5 0.0 copy-done.2
  126.5 1.1 fusion.1
  127.6 0.0 copy-done
  127.6 1.0 copy.15
  (5 shorter events, 0.0 us)
Async XLA Ops:
  99.7 20.3 %collective-permute-start = (bf16[4,256,256]{2,1,0:T(8,128)(2,1)}, bf16[4,256,256]{2,1,0:T(8,128)(2,1)S(1)}, u32[]{:S(2)}, u32[]{:S(2)}) collective-permute-start(bf16[4,256,256]{2,1,0:T(8,128)(2,1)} %get-tuple-element.12), channel_id=1, source_target_pairs={{0,8},{8,0},{16,24},{24,16},{1,9},{9,1},{17,25},{25,17},{2,10},{10... | collective-permute-start | bytes 1572872 | tf_op jit(solution)/shard_map/ppermute | solution.py:288
  101.2 25.4 %collective-permute-start.1 = (bf16[4,256,256]{2,1,0:T(8,128)(2,1)}, bf16[4,256,256]{2,1,0:T(8,128)(2,1)S(1)}, u32[]{:S(2)}, u32[]{:S(2)}) collective-permute-start(bf16[4,256,256]{2,1,0:T(8,128)(2,1)} %get-tuple-element.13), channel_id=1, source_target_pairs={{0,16},{8,24},{16,0},{24,8},{1,17},{9,25},{17,1},{25,9},{2,18},{10... | collective-permute-start | bytes 1572872 | tf_op jit(solution)/shard_map/ppermute | solution.py:288
  102.7 23.8 %collective-permute-start.2 = (bf16[4,256,256]{2,1,0:T(8,128)(2,1)}, bf16[4,256,256]{2,1,0:T(8,128)(2,1)S(1)}, u32[]{:S(2)}, u32[]{:S(2)}) collective-permute-start(bf16[4,256,256]{2,1,0:T(8,128)(2,1)} %get-tuple-element.14), channel_id=1, source_target_pairs={{0,24},{8,16},{16,8},{24,0},{1,25},{9,17},{17,9},{25,1},{2,26},{10... | collective-permute-start | bytes 1572872 | tf_op jit(solution)/shard_map/ppermute | solution.py:288
  103.2 23.4 %copy-start.1 = (bf16[1,4,256,256]{3,2,1,0:T(8,128)(2,1)S(1)}, bf16[1,4,256,256]{3,2,1,0:T(8,128)(2,1)}, u32[]{:S(2)}) copy-start(bf16[1,4,256,256]{3,2,1,0:T(8,128)(2,1)} %param.11) | copy-start | bytes 1572868
  103.2 23.4 %copy-start.2 = (bf16[4,256,256]{2,1,0:T(8,128)(2,1)S(1)}, bf16[4,256,256]{2,1,0:T(8,128)(2,1)}, u32[]{:S(2)}) copy-start(bf16[4,256,256]{2,1,0:T(8,128)(2,1)} %get-tuple-element.11) | copy-start | bytes 1572868
  103.2 24.5 %copy-start = (bf16[1024,512]{1,0:T(8,128)(2,1)S(1)}, bf16[1024,512]{1,0:T(8,128)(2,1)}, u32[]{:S(2)}) copy-start(bf16[1024,512]{1,0:T(8,128)(2,1)} %get-tuple-element.9) | copy-start | bytes 3145732

commit v2 on v1

--- a/solution.py
+++ b/solution.py
@@ -8,6 +8,7 @@
 from jax.sharding import PartitionSpec as P
 
 NB = 128
+AT_ONCE = 4
 MESH = pl.DeviceIdType.MESH
 HI = lax.Precision.HIGHEST
 VMEM_LIMIT = 56 * 1024 * 1024
@@ -26,24 +27,33 @@
     col = lax.broadcasted_iota(jnp.int32, (NB, NB), 1)
     e = jnp.where(row == col, 1.0, 0.0).astype(jnp.float32)
     top = 0
-    for j in range(NB):
+    for j in range(0, NB, AT_ONCE):
         if j - top == 16:
             d, e, top = d[16:], e[16:], j
         if j == NB // 2:
             midway()
         r = j - top
-        drow = d[r:r + 1, :]
-        erow = e[r:r + 1, :]
-        pivot = jnp.broadcast_to(drow[:, j:j + 1], (1, NB))
-        inv_ref[j:j + 1, :] = erow * lax.rsqrt(pivot)
-        inverse = 1.0 / pivot
-        factor = jnp.broadcast_to(d[:, j:j + 1], d.shape)
-        d = d - factor * (drow * inverse)
-        e = e - factor * (erow * inverse)
+        drow = [d[r + i:r + i + 1, :] for i in range(AT_ONCE)]
+        erow = [e[r + i:r + i + 1, :] for i in range(AT_ONCE)]
+        factor = [jnp.broadcast_to(d[:, j + i:j + i + 1], d.shape) for i in range(AT_ONCE)]
+        for i in range(AT_ONCE):
+            pivot = factor[i][r + i:r + i + 1, :]
+            inv_ref[j + i:j + i + 1, :] = erow[i] * lax.rsqrt(pivot)
+            inverse = 1.0 / pivot
+            drow[i] = drow[i] * inverse
+            erow[i] = erow[i] * inverse
+            for k in range(i + 1, AT_ONCE):
+                below = factor[i][r + k:r + k + 1, :]
+                drow[k] = drow[k] - below * drow[i]
+                erow[k] = erow[k] - below * erow[i]
+                factor[k] = factor[k] - factor[i] * (factor[k][r + i:r + i + 1, :] * inverse)
+        for i in range(AT_ONCE):
+            d = d - factor[i] * drow[i]
+            e = e - factor[i] * erow[i]
 
 
 def factor_kernel(
-    stages, s_in, a_in, x_all, panel_out, s_ref, a_ref, inv_ref, x_ref,
+    stages, s_in, a_in, x_all, s_ref, a_ref, inv_ref, x_ref,
     own_sem, net_send, down_send, net_recv, part_send, part_recv,
 ):
     leaf, blk = lax.axis_index("leaf"), lax.axis_index("blk")
@@ -137,9 +147,7 @@
         eliminate(s_now[at:at + NB, at:at + NB], inv_ref, lambda: forwards(2 * q - 1))
         inverse = inv_ref[...]
         x = mm(a_now[:, at:at + NB], inverse, (1, 1))
-        rounded = x.astype(x_ref.dtype)
-        x_ref[q] = rounded.reshape(count, width, NB)
-        panel_out[:, at:at + NB] = rounded
+        x_ref[q] = x.astype(x_ref.dtype).reshape(count, width, NB)
         if q == 0:
             pl.semaphore_wait(barrier, 1 + jnp.minimum(z, 1) + jnp.minimum(last - z, 1))
 
@@ -180,12 +188,9 @@
     dma = pltpu.SemaphoreType.DMA
     return pl.pallas_call(
         functools.partial(factor_kernel, stages),
-        out_shape=[
-            jax.ShapeDtypeStruct((slices, parts * count, width, NB), jnp.bfloat16),
-            jax.ShapeDtypeStruct((rows, order), jnp.bfloat16),
-        ],
+        out_shape=jax.ShapeDtypeStruct((slices, parts * count, width, NB), jnp.bfloat16),
         in_specs=[vmem, vmem],
-        out_specs=[pl.BlockSpec(memory_space=pl.ANY), vmem],
+        out_specs=pl.BlockSpec(memory_space=pl.ANY),
         scratch_shapes=[
             pltpu.VMEM((order, order), jnp.float32),
             pltpu.VMEM((rows, order), jnp.float32),
@@ -214,37 +219,47 @@
     return jnp.where(live, mm(left, right, (1, 1), None), 0.0)
 
 
-def top_kernel(pairs, rows, *outs):
+def top_kernel(pairs, pattern, rows, *outs):
     per_out = outs[0].shape[0]
+    leaf = lax.axis_index("leaf")
     for k in range(len(outs)):
+        base = (leaf ^ k) * per_out
         for s in range(per_out):
-            at = k * per_out + s
-            outs[k][s] = product(rows, pairs[0, at], pairs[1, at]).astype(outs[k].dtype)
-
-
-def run_top(pairs, rows, shares, width):
+            p, q = pattern[0, pairs[0, base + s]], pattern[0, pairs[1, base + s]]
+            outs[k][s] = product(rows, p, q).astype(outs[k].dtype)
+
+
+def run_top(pairs, pattern, rows, shares, width):
     per_out = pairs.shape[1] // shares
     vmem = pl.BlockSpec(memory_space=pltpu.VMEM)
     shape = jax.ShapeDtypeStruct((per_out, width, width), jnp.bfloat16)
     return pl.pallas_call(
         top_kernel,
-        in_specs=[pl.BlockSpec(memory_space=pltpu.SMEM), vmem],
+        in_specs=[pl.BlockSpec(memory_space=pltpu.SMEM)] * 2 + [vmem],
         out_specs=[vmem] * shares,
         out_shape=[shape] * shares,
         compiler_params=pltpu.CompilerParams(vmem_limit_bytes=VMEM_LIMIT),
         cost_estimate=pl.CostEstimate(flops=1_000_000_000, bytes_accessed=10_000_000, transcendentals=0),
         name="top_products",
-    )(pairs, rows)
-
-
-def local_kernel(per_step, pairs, rows, target, out):
+    )(pairs, pattern, rows)
+
+
+def local_kernel(per_step, pairs, rows, target, out, own):
     base = pl.program_id(0) * per_step
+
+    @pl.when(base == 0)
+    def _():
+        first = lax.axis_index("blk") * own.shape[0]
+        for i in range(own.shape[0]):
+            for k in range(rows.shape[0]):
+                own[i, :, k * NB:(k + 1) * NB] = rows[k, first + i]
+
     for s in range(per_step):
         fresh = target[s].astype(jnp.float32) - product(rows, pairs[0, base + s], pairs[1, base + s])
         out[s] = fresh.astype(out.dtype)
 
 
-def run_local(pairs, rows, targets, per_step):
+def run_local(pairs, rows, targets, own_count, per_step):
     count, width = targets.shape[:2]
     depth = rows.shape[0] * rows.shape[3]
     whole = pl.BlockSpec(rows.shape, lambda i, pairs: (0, 0, 0, 0), pipeline_mode=pl.Buffered(1))
@@ -255,9 +270,12 @@
             num_scalar_prefetch=1,
             grid=(count // per_step,),
             in_specs=[whole, block],
-            out_specs=block,
+            out_specs=[block, pl.BlockSpec((own_count, width, depth), lambda i, pairs: (0, 0, 0))],
         ),
-        out_shape=jax.ShapeDtypeStruct((count, width, width), jnp.bfloat16),
+        out_shape=[
+            jax.ShapeDtypeStruct((count, width, width), jnp.bfloat16),
+            jax.ShapeDtypeStruct((own_count, width, depth), jnp.bfloat16),
+        ],
         compiler_params=pltpu.CompilerParams(vmem_limit_bytes=VMEM_LIMIT),
         cost_estimate=pl.CostEstimate(
             flops=2 * count * width * width * depth,
@@ -272,28 +290,18 @@
     s = diag_blocks[0]
     count, width, columns = panel.shape[1:]
     a = panel[0].reshape(count * width, columns)
-    pattern = top_pattern[0]
-    ancestors = jnp.arange(pattern.shape[0], dtype=jnp.int32)
-
-    def lookup(ids):
-        return jnp.sum(jnp.where(ids[:, None] == ancestors[None, :], pattern[None, :], 0), axis=1)
-
-    owners = lax.axis_index("leaf") ^ jnp.arange(leaves, dtype=jnp.int32)
-    pairs_by_share = top_pairs[0].reshape(leaves, -1, 2)[owners].reshape(-1, 2)
-    positions = jnp.stack([lookup(pairs_by_share[:, 0]), lookup(pairs_by_share[:, 1])])
-
-    rows, panel_out = run_factor(s, a, count, parts)
-    shares = run_top(positions, rows, leaves, width)
+    rows = run_factor(s, a, count, parts)
+    shares = run_top(top_pairs[0].T, top_pattern, rows, leaves, width)
     arrived = [
         lax.ppermute(shares[m], "leaf", [(i, i ^ m) for i in range(leaves)])
         for m in range(1, leaves)
     ]
-    updated = run_local(local_pairs[0].T, rows, local_targets[0], 8)
+    updated, panel_out = run_local(local_pairs[0].T, rows, local_targets[0], count, 8)
     summed = shares[0].astype(jnp.float32)
     for term in arrived:
         summed = summed + term.astype(jnp.float32)
     top_out = (top_targets[0].astype(jnp.float32) - summed).astype(jnp.bfloat16)[None]
-    return (panel_out.reshape(panel.shape), updated[None], top_out)
+    return (panel_out[None], updated[None], top_out)
 
 
 def solution(mesh):

time: 129 us -> 117 us (0.907)
  Pallas kernels: 113 us -> 105 us
  local copies, waits for them, and re-layouts: 2.42 us -> 0.01 us
  other arithmetic: 2.55 us -> 1.12 us
    pallas_call x1, Pallas kernels: 90.4 us -> 82.8 us  [run_factor(): pl.pallas_call(functools.partial(factor_kernel, stages), out_shape=jax.Sh...]
  transfers between devices with their start and end apart: 3 -> 3, of which waited for: 1 -> 1; matrix products, arithmetic and copies ran while one was open for 0% -> 0% of each run, Pallas kernels for 13% -> 15%
where the time goes in v2:
time: 117 us
  Pallas kernels  105 us (90%)
  waiting for transfers between devices  6.37 us (5%)
  starting transfers between devices  3.5 us (3%)
    pallas_call x1, Pallas kernels, run_factor(): pl.pallas_call(functools.partial(factor_kernel, stages), out_shape=jax.Sh...  82.8 us
    pallas_call x1, Pallas kernels, run_local(): pl.pallas_call(functools.partial(local_kernel, per_step), grid_spec=pltpu...  17 us
    ppermute x3, waiting for transfers between devices, on_device(): lax.ppermute(shares[m], 'leaf', [(i, i ^ m) for i in range(leaves)])  6.37 us
    pallas_call x1, Pallas kernels, run_top(): pl.pallas_call(top_kernel, in_specs=[pl.BlockSpec(memory_space=pltpu.SMEM...  5.62 us
    ppermute x3, starting transfers between devices, on_device(): lax.ppermute(shares[m], 'leaf', [(i, i ^ m) for i in range(leaves)])  3.5 us
  transfers between devices with their start and end apart: 3, of which 1 were waited for; matrix products, arithmetic and copies ran while one was open for 0% of the time, Pallas kernels for 15%

profile of v2, /device:TPU:0, one launch (start us, length us, event | category | flops | bytes accessed | tf_op | source)
XLA Modules:
  0.0 117.1 jit_solution(16946118226648553687)
XLA Ops:
  0.6 82.8 %factor_and_gather.1.rows = bf16[4,32,256,128]{3,2,1,0:T(8,128)(2,1)} custom-call(f32[512,512]{1,0:T(8,128)} %bitcast.19, f32[1024,512]{1,0:T(8,128)} %bitcast.18), custom_call_target="tpu_custom_call" | custom-call | flops 80000000000 | bytes 16000000 | tf_op jit(solution)/shard_map/factor_and_gather/pallas_call | solution.py:189
  83.5 5.6 %top_products.1 = (bf16[4,256,256]{2,1,0:T(8,128)(2,1)}, bf16[4,256,256]{2,1,0:T(8,128)(2,1)}, bf16[4,256,256]{2,1,0:T(8,128)(2,1)}, bf16[4,256,256]{2,1,0:T(8,128)(2,1)}) custom-call(s32[2,16]{1,0:T(2,128)} %bitcast.16, s32[1,64]{1,0:T(1,128)} %pattern.1, bf16[4,32,256,128]{3,2,1,0:T(8,128)(2,1)} %factor_and_gather.1.rows), custom_call_target="tpu_custom_call" | custom-call | flops 1000000000 | bytes 10000000 | tf_op jit(solution)/shard_map/top_products/pallas_call | solution.py:236
  89.1 0.0 copy-start
  89.1 0.0 copy-start.1
  89.1 1.5 %collective-permute-start = (bf16[4,256,256]{2,1,0:T(8,128)(2,1)}, bf16[4,256,256]{2,1,0:T(8,128)(2,1)S(1)}, u32[]{:S(2)}, u32[]{:S(2)}) collective-permute-start(bf16[4,256,256]{2,1,0:T(8,128)(2,1)} %get-tuple-element.12), channel_id=1, source_target_pairs={{0,8},{8,0},{16,24},{24,16},{1,9},{9,1},{17,25},{25,17},{2,10},{10... | collective-permute-start | bytes 1572872 | tf_op jit(solution)/shard_map/ppermute | solution.py:296
  90.6 1.5 %collective-permute-start.1 = (bf16[4,256,256]{2,1,0:T(8,128)(2,1)}, bf16[4,256,256]{2,1,0:T(8,128)(2,1)S(1)}, u32[]{:S(2)}, u32[]{:S(2)}) collective-permute-start(bf16[4,256,256]{2,1,0:T(8,128)(2,1)} %get-tuple-element.13), channel_id=1, source_target_pairs={{0,16},{8,24},{16,0},{24,8},{1,17},{9,25},{17,1},{25,9},{2,18},{10... | collective-permute-start | bytes 1572872 | tf_op jit(solution)/shard_map/ppermute | solution.py:296
  92.1 0.5 collective-permute-start.2
  92.6 17.0 %local_updates.1 = (bf16[80,256,256]{2,1,0:T(8,128)(2,1)}, bf16[4,256,512]{2,1,0:T(8,128)(2,1)}) custom-call(s32[2,80]{1,0:T(2,128)} %bitcast.20, bf16[4,32,256,128]{3,2,1,0:T(8,128)(2,1)} %factor_and_gather.1.rows, bf16[80,256,256]{2,1,0:T(8,128)(2,1)} %bitcast.17), custom_call_target="tpu_custom_call" | custom-call | flops 5368709120 | bytes 20971520 | tf_op jit(solution)/shard_map/local_updates/pallas_call | solution.py:267
  109.6 0.0 collective-permute-done
  109.6 6.4 %collective-permute-done.1 = bf16[4,256,256]{2,1,0:T(8,128)(2,1)S(1)} collective-permute-done((bf16[4,256,256]{2,1,0:T(8,128)(2,1)}, bf16[4,256,256]{2,1,0:T(8,128)(2,1)S(1)}, u32[]{:S(2)}, u32[]{:S(2)}) %collective-permute-start.1) | collective-permute-done | bytes 524320 | tf_op jit(solution)/shard_map/ppermute | solution.py:296
  115.9 0.0 collective-permute-done.2
  115.9 0.0 copy-done
  115.9 0.0 copy-done.1
  115.9 1.1 fusion.1
Async XLA Ops:
  89.1 26.9 %copy-start = (bf16[1,4,256,256]{3,2,1,0:T(8,128)(2,1)S(1)}, bf16[1,4,256,256]{3,2,1,0:T(8,128)(2,1)}, u32[]{:S(2)}) copy-start(bf16[1,4,256,256]{3,2,1,0:T(8,128)(2,1)} %param.11) | copy-start | bytes 1572868
  89.1 26.9 %copy-start.1 = (bf16[4,256,256]{2,1,0:T(8,128)(2,1)S(1)}, bf16[4,256,256]{2,1,0:T(8,128)(2,1)}, u32[]{:S(2)}) copy-start(bf16[4,256,256]{2,1,0:T(8,128)(2,1)} %get-tuple-element.11) | copy-start | bytes 1572868
  89.1 20.5 %collective-permute-start = (bf16[4,256,256]{2,1,0:T(8,128)(2,1)}, bf16[4,256,256]{2,1,0:T(8,128)(2,1)S(1)}, u32[]{:S(2)}, u32[]{:S(2)}) collective-permute-start(bf16[4,256,256]{2,1,0:T(8,128)(2,1)} %get-tuple-element.12), channel_id=1, source_target_pairs={{0,8},{8,0},{16,24},{24,16},{1,9},{9,1},{17,25},{25,17},{2,10},{10... | collective-permute-start | bytes 1572872 | tf_op jit(solution)/shard_map/ppermute | solution.py:296
  90.6 25.4 %collective-permute-start.1 = (bf16[4,256,256]{2,1,0:T(8,128)(2,1)}, bf16[4,256,256]{2,1,0:T(8,128)(2,1)S(1)}, u32[]{:S(2)}, u32[]{:S(2)}) collective-permute-start(bf16[4,256,256]{2,1,0:T(8,128)(2,1)} %get-tuple-element.13), channel_id=1, source_target_pairs={{0,16},{8,24},{16,0},{24,8},{1,17},{9,25},{17,1},{25,9},{2,18},{10... | collective-permute-start | bytes 1572872 | tf_op jit(solution)/shard_map/ppermute | solution.py:296
  92.1 23.8 %collective-permute-start.2 = (bf16[4,256,256]{2,1,0:T(8,128)(2,1)}, bf16[4,256,256]{2,1,0:T(8,128)(2,1)S(1)}, u32[]{:S(2)}, u32[]{:S(2)}) collective-permute-start(bf16[4,256,256]{2,1,0:T(8,128)(2,1)} %get-tuple-element.14), channel_id=1, source_target_pairs={{0,24},{8,16},{16,8},{24,0},{1,25},{9,17},{17,9},{25,1},{2,26},{10... | collective-permute-start | bytes 1572872 | tf_op jit(solution)/shard_map/ppermute | solution.py:296
